TPU v7x, 32 devices: a whole 2x2x4 slice. The times are simulated.
32 devices in a mesh: parts: 2 (over y), dp: 8 (over z, x), mp: 2 (over core).
Axes of the slice: x: 2, y: 2, z: 4, core: 2. Of those that a mesh axis runs over, the one named last changes fastest.
Arguments:
- embeddings: bfloat16 [6144, 1024], P(('parts', 'dp'), 'mp'), parts along dimension 0, may hold values from -6 to 6
- labels: int32 [6144], P(('parts', 'dp')), parts along dimension 0, may hold values from 0 to 1023, as said below
- block_lists: int32 [2048, 2], P(('parts', 'dp')), parts along dimension 0, may hold values from -1 to 3, as said below
- level1: bfloat16 [16384, 1024], P(('parts', 'dp'), 'mp'), parts along dimension 0, may hold values from -6 to 6
- level2: bfloat16 [2048, 1024], P(('parts', 'dp'), 'mp'), parts along dimension 0, may hold values from -6 to 6
- level3: bfloat16 [512, 1024], P('parts', 'mp'), parts along dimension 0, may hold values from -6 to 6
Outputs:
- new_level1: bfloat16 [16384, 1024], P(('parts', 'dp'), 'mp'), parts along dimension 0
- new_level2: bfloat16 [2048, 1024], P(('parts', 'dp'), 'mp'), parts along dimension 0
- new_level3: bfloat16 [512, 1024], P('parts', 'mp'), parts along dimension 0
There are 2 independent parts, one for each index of `parts`. A program takes and returns all parts, laid end to end along the dimension named above; each array names one. Nothing has to cross between parts.
Inputs may be any that keep to these rules, and one draw needn't show every extreme that they name: Among the 384 embeddings of one index of dp, at most 96 have labels of one owner (label // 128), and exactly 96 for some owner on every index. `block_lists`: each row holds distinct block numbers followed by -1 padding; its first entry is never -1.
All inputs are finite; a program needn't handle non-finite values.
Results may differ from a plain program's by a relative error of at most 0.004.
Values may be sent and summed in bfloat16 or wider, within the bound.
A program may use at most 64 MiB of HBM per device.

v0:
```python
import jax
import jax.numpy as jnp
from jax import lax
from jax.sharding import PartitionSpec as P

E = 1024
BR = 256
BLK_DEV = 4


def soft_weights(scores, mask):
    top = jnp.max(jnp.where(mask, scores, -1e30), axis=1, keepdims=True)
    expd = jnp.where(mask, jnp.exp(scores - top), 0.0)
    total = jnp.sum(expd, axis=1, keepdims=True)
    total = jnp.where(total > 0, total, 1.0)
    return (expd / total).astype(jnp.bfloat16)


def shards(embeddings, labels, block_lists, level1, level2, level3):
    scale = float(E) ** (-0.5)
    groups = lax.axis_size("dp")
    rows, half = embeddings.shape
    k2_local = level2.shape[0]
    cap = max(2, 2 * rows // groups)
    slots = groups * cap
    dest = labels // k2_local
    dest_hot = (dest[:, None] == jnp.arange(groups)[None, :]).astype(jnp.int32)
    rank = jnp.sum(dest_hot * (jnp.cumsum(dest_hot, axis=0) - 1), axis=1)
    target = dest * cap + rank
    sent_rows = jnp.zeros((slots, half), jnp.bfloat16).at[target].set(embeddings)
    sent_labels = jnp.full((slots,), -1, jnp.int32).at[target].set(labels - dest * k2_local)
    got_rows, got_labels = (
        lax.all_to_all(
            sent_rows.reshape(groups, cap, half), "dp", split_axis=0, concat_axis=0, tiled=True
        ),
        lax.all_to_all(
            sent_labels.reshape(groups, cap), "dp", split_axis=0, concat_axis=0, tiled=True
        ),
    )
    got_rows = got_rows.reshape(slots, half)
    got_labels = got_labels.reshape(slots)
    label_hot = got_labels[:, None] == jnp.arange(k2_local)[None, :]
    listed = jnp.any(block_lists[:, :, None] == jnp.arange(BLK_DEV)[None, None, :], axis=1).astype(
        jnp.float32
    )
    allowed = jnp.dot(label_hot.astype(jnp.float32), listed) > 0.5
    mask = jnp.repeat(allowed, BR, axis=1)
    cent_f = level1.astype(jnp.float32)
    norms = jnp.sum(cent_f * cent_f, axis=1)
    partial_value = (
        jnp.dot(got_rows, level1.T, preferred_element_type=jnp.float32) - 0.5 * norms[None, :]
    )
    scores = lax.psum(partial_value, "mp") * scale
    resp = soft_weights(scores, mask)
    num = jnp.dot(resp.T, got_rows, preferred_element_type=jnp.float32)
    weight = jnp.sum(resp.astype(jnp.float32), axis=0)
    new_level1 = ((num + cent_f) / (weight + 1.0)[:, None]).astype(jnp.bfloat16)
    member = label_hot.astype(jnp.bfloat16)
    sums = jnp.dot(member.T, got_rows, preferred_element_type=jnp.float32)
    count = jnp.sum(label_hot.astype(jnp.float32), axis=0)
    new_level2 = ((sums + level2.astype(jnp.float32)) / (count + 1.0)[:, None]).astype(jnp.bfloat16)
    third = level3.astype(jnp.float32)
    norms3 = jnp.sum(third * third, axis=1)
    partial3 = (
        jnp.dot(new_level2, level3.T, preferred_element_type=jnp.float32) - 0.5 * norms3[None, :]
    )
    scores3 = lax.psum(partial3, "mp") * scale
    resp3 = jax.nn.softmax(scores3, axis=1).astype(jnp.bfloat16)
    num3 = jnp.dot(resp3.T, new_level2, preferred_element_type=jnp.float32)
    weight3 = jnp.sum(resp3.astype(jnp.float32), axis=0)
    total3, mass3 = lax.psum((num3, weight3), "dp")
    new_level3 = ((total3 + third) / (mass3 + 1.0)[:, None]).astype(jnp.bfloat16)
    return (new_level1, new_level2, new_level3)


def solution(mesh):
    return jax.shard_map(
        shards,
        mesh=mesh,
        in_specs=(
            P(("parts", "dp"), "mp"),
            P(("parts", "dp")),
            P(("parts", "dp"), None),
            P(("parts", "dp"), "mp"),
            P(("parts", "dp"), "mp"),
            P("parts", "mp"),
        ),
        out_specs=(P(("parts", "dp"), "mp"), P(("parts", "dp"), "mp"), P("parts", "mp")),
        check_vma=False,
    )
```

profile of v0, /device:TPU:0, one launch (start us, length us, event | category | flops | bytes accessed | tf_op | source)
XLA Modules:
  0.0 162.7 jit_solution(2593100775157816182)
XLA Ops:
  7.2 0.0 copy-start.3
  7.2 0.8 multiply_subtract_fusion
  8.0 0.9 reduce-window.6
  8.8 0.2 slice_reduce_fusion
  9.1 0.1 fusion.14
  9.2 2.9 %scatter_custom_fusion = s32[768]{0:T(1024)S(1)} fusion(s32[384]{0:T(512)S(1)} %compare_select_fusion.1, s32[384]{0:T(512)S(1)} %get-tuple-element.9, s32[]{:T(128)} %constant.16.clone.1), kind=kCustom, calls=%fused_computation.53 | custom fusion | bytes 3076 | tf_op jit(solution)/shard_map/scatter | solution.py:31
  12.1 0.7 all_to_all.9
  12.8 7.3 %all-to-all-start = ((s32[8,1,96]{2,1,0:T(1,128)}), s32[8,1,96]{2,1,0:T(1,128)S(1)}, u32[]{:S(2)}, u32[]{:S(2)}) async-start(s32[8,1,96]{2,1,0:T(1,128)} %all_to_all.9), calls=%async_computation | async-start | bytes 8192 | tf_op jit(solution)/shard_map/all_to_all | solution.py:36
  20.0 3.3 %scatter_custom_fusion.1 = bf16[768,512]{1,0:T(8,128)(2,1)} fusion(s32[384]{0:T(512)S(1)} %compare_select_fusion.1, bf16[384,512]{1,0:T(8,128)(2,1)} %param.6, bf16[]{:T(256)} %constant.12.clone.1), kind=kCustom, calls=%fused_computation.24 | custom fusion | bytes 786944 | tf_op jit(solution)/shard_map/scatter | solution.py:30
  23.4 3.1 %all-to-all-done = s32[8,1,96]{2,1,0:T(1,128)S(1)} async-done(((s32[8,1,96]{2,1,0:T(1,128)}), s32[8,1,96]{2,1,0:T(1,128)S(1)}, u32[]{:S(2)}, u32[]{:S(2)}) %all-to-all-start) | async-done | bytes 3104 | tf_op jit(solution)/shard_map/all_to_all | solution.py:36
  26.4 3.5 %all-to-all-start.1 = ((bf16[8,96,512]{2,1,0:T(8,128)(2,1)}), bf16[8,96,512]{2,1,0:T(8,128)(2,1)S(1)}, u32[]{:S(2)}, u32[]{:S(2)}) async-start(bf16[8,96,512]{2,1,0:T(8,128)(2,1)} %bitcast.3), calls=%async_computation.1 | async-start | bytes 1572864 | tf_op jit(solution)/shard_map/all_to_all | solution.py:33
  30.0 0.0 all-reduce.6.cloned.1.call-start
  30.0 1.1 fusion.6
  31.1 0.0 copy-done.3
  31.1 0.3 fusion
  31.4 0.0 copy-start.8
  31.4 0.5 broadcast.85
  32.0 0.7 reduce.5
  32.6 0.1 eq.58
  32.7 0.2 convert_reduce_fusion.1
  32.9 16.2 %all-to-all-done.1 = bf16[8,96,512]{2,1,0:T(8,128)(2,1)S(1)} async-done(((bf16[8,96,512]{2,1,0:T(8,128)(2,1)}), bf16[8,96,512]{2,1,0:T(8,128)(2,1)S(1)}, u32[]{:S(2)}, u32[]{:S(2)}) %all-to-all-start.1) | async-done | bytes 786464 | tf_op jit(solution)/shard_map/all_to_all | solution.py:33
  49.1 0.0 copy-start.5
  49.1 0.0 copy-start.2
  49.1 2.7 %convolution_subtract_fusion = f32[768,1024]{1,0:T(8,128)} fusion(bf16[768,512]{1,0:T(8,128)(2,1)S(1)} %bitcast.26, bf16[1024,512]{1,0:T(8,128)(2,1)S(1)} %copy-done.3, f32[1024]{0:T(1024)S(1)} %broadcast_multiply_fusion), kind=kOutput, calls=%fused_computation.12 | convolution fusion | flops 806092800 | bytes 4984832 | tf_op jit(solution)/shard_map/dot_general | solution.py:51
  51.8 0.0 copy-done.8
  51.8 0.0 copy-start.9
  51.8 0.5 fusion.5
  52.3 0.0 copy-done.5
  52.3 0.0 copy-done.2
  52.3 0.0 copy-start.7
  52.3 0.9 convolution_subtract_fusion.1
  53.2 0.0 all-reduce.6.cloned.1.call-update
  53.2 0.0 all-reduce.4.cloned.1.call-start
  53.3 0.0 copy-done.9
  53.3 0.3 convolution_compare_fusion
  53.6 0.3 copy.13
  53.8 1.1 broadcast_in_dim.21
  55.0 1.3 copy.14
  56.3 19.6 %all-reduce.6.cloned.1.call-done = (f32[768,1024]{1,0:T(8,128)}, f32[128,256]{1,0:T(8,128)}) async-done(((f32[768,1024]{1,0:T(8,128)}, f32[128,256]{1,0:T(8,128)}), (f32[768,1024]{1,0:T(8,128)}, f32[128,256]{1,0:T(8,128)})) %all-reduce.6.cloned.1.call-update) | async-done | bytes 3276816 | tf_op jit(solution)/shard_map/psum | solution.py:53
  75.9 0.0 copy-start
  75.9 1.2 multiply_reduce_fusion
  77.1 1.1 fusion.13
  78.1 1.0 convert_reduce_fusion.2
  79.2 0.0 copy-done.7
  79.2 1.1 fusion.21
  80.3 0.0 all-reduce.4.cloned.1.call-update
  80.3 21.7 %psum.31 = f32[256]{0:T(256)S(1)} all-reduce(f32[256]{0:T(256)S(1)} %get-tuple-element.5), channel_id=1, replica_groups=mesh['parts'=2,'dp'=8,'mp'=2] {'dp'}, use_global_device_ids=true, to_apply=%region_18.19 | all-reduce | flops 256 | bytes 2048 | tf_op jit(solution)/shard_map/psum | solution.py:71
  102.0 0.0 copy-start.1
  102.0 2.8 %select_reduce_fusion = f32[768]{0:T(1024)S(1)} fusion(pred[768,1024]{1,0:T(8,128)(4,1)} %bitcast.22, f32[768,1024]{1,0:T(8,128)} %get-tuple-element.3), kind=kLoop, calls=%fused_computation.5 | loop fusion | flops 2358528 | bytes 3935232 | tf_op jit(solution)/shard_map/reduce_max | solution.py:12
  104.8 0.0 copy-done
  104.8 0.0 copy-done.1
  104.8 1.0 fusion.3
  105.8 0.0 copy-start.4
  105.8 0.0 copy-start.6
  105.9 1.1 convert_reduce_fusion
  106.9 0.1 copy-done.4
  107.1 0.2 copy-done.6
  107.3 2.0 %fusion.2 = bf16[1024,512]{1,0:T(8,128)(2,1)} fusion(bf16[1024,512]{1,0:T(8,128)(2,1)S(1)} %copy-done.4, bf16[768,1024]{1,0:T(8,128)(2,1)S(1)} %get-tuple-element.8, bf16[768,512]{1,0:T(8,128)(2,1)S(1)} %bitcast.28, f32[1024]{0:T(1024)S(1)} %broadcast_add_fusion), kind=kOutput, calls=%fused_computation.10 | convolution fusion | flops 807403520 | bytes 4460544 | tf_op jit(solution)/shard_map/dot_general | solution.py:55
  109.3 44.7 %all-reduce.4.cloned.1.call-done = f32[256,512]{1,0:T(8,128)} async-done(((f32[256,512]{1,0:T(8,128)}), f32[256,512]{1,0:T(8,128)}) %all-reduce.4.cloned.1.call-update) | async-done | bytes 524304 | tf_op jit(solution)/shard_map/psum | solution.py:71
  154.0 1.9 %fusion.8 = bf16[256,512]{1,0:T(8,128)(2,1)} fusion(f32[256,512]{1,0:T(8,128)} %all-reduce.4.cloned.1.call-done, bf16[256,512]{1,0:T(8,128)(2,1)S(1)} %copy-done.2, f32[256]{0:T(256)S(1)} %broadcast_add_fusion.1), kind=kLoop, calls=%fused_computation.22 | loop fusion | flops 524288 | bytes 1049600 | tf_op jit(solution)/shard_map/convert_element_type | solution.py:72
  (10 shorter events, 0.1 us)
Async XLA Ops:
  7.2 24.0 %copy-start.3 = (bf16[1024,512]{1,0:T(8,128)(2,1)S(1)}, bf16[1024,512]{1,0:T(8,128)(2,1)}, u32[]{:S(2)}) copy-start(bf16[1024,512]{1,0:T(8,128)(2,1)} %param.9) | copy-start | bytes 3145732
  12.8 13.6 %all-to-all-start = ((s32[8,1,96]{2,1,0:T(1,128)}), s32[8,1,96]{2,1,0:T(1,128)S(1)}, u32[]{:S(2)}, u32[]{:S(2)}) async-start(s32[8,1,96]{2,1,0:T(1,128)} %all_to_all.9), calls=%async_computation | async-start | bytes 8192 | tf_op jit(solution)/shard_map/all_to_all | solution.py:36
  26.4 22.6 %all-to-all-start.1 = ((bf16[8,96,512]{2,1,0:T(8,128)(2,1)}), bf16[8,96,512]{2,1,0:T(8,128)(2,1)S(1)}, u32[]{:S(2)}, u32[]{:S(2)}) async-start(bf16[8,96,512]{2,1,0:T(8,128)(2,1)} %bitcast.3), calls=%async_computation.1 | async-start | bytes 1572864 | tf_op jit(solution)/shard_map/all_to_all | solution.py:33
  30.0 45.9 %all-reduce.6.cloned.1.call-start = ((), (), s32[]{:S(2)}) async-start(), calls=%async_computation.3 | async-start | bytes 6553600 | tf_op jit(solution)/shard_map/psum | solution.py:53
  31.4 20.4 %copy-start.8 = (bf16[128,512]{1,0:T(8,128)(2,1)S(1)}, bf16[128,512]{1,0:T(8,128)(2,1)}, u32[]{:S(2)}) copy-start(bf16[128,512]{1,0:T(8,128)(2,1)} %param.10) | copy-start | bytes 393220
  49.1 3.2 %copy-start.5 = (bf16[8,96,512]{2,1,0:T(8,128)(2,1)}, bf16[8,96,512]{2,1,0:T(8,128)(2,1)S(1)}, u32[]{:S(2)}) copy-start(bf16[8,96,512]{2,1,0:T(8,128)(2,1)S(1)} %all-to-all-done.1) | copy-start | bytes 2359300
  49.1 3.2 %copy-start.2 = (bf16[256,512]{1,0:T(8,128)(2,1)S(1)}, bf16[256,512]{1,0:T(8,128)(2,1)}, u32[]{:S(2)}) copy-start(bf16[256,512]{1,0:T(8,128)(2,1)} %param.11) | copy-start | bytes 786436
  51.8 1.5 copy-start.9
  52.3 26.9 %copy-start.7 = (bf16[128,512]{1,0:T(8,128)(2,1)}, bf16[128,512]{1,0:T(8,128)(2,1)S(1)}, u32[]{:S(2)}) copy-start(bf16[128,512]{1,0:T(8,128)(2,1)S(1)} %fusion.5) | copy-start | bytes 393220
  53.2 100.8 %all-reduce.4.cloned.1.call-start = ((), (), s32[]{:S(2)}) async-start(), calls=%async_computation.2 | async-start | bytes 1048576 | tf_op jit(solution)/shard_map/psum | solution.py:71
  75.9 28.9 %copy-start = (f32[768,1024]{1,0:T(8,128)S(1)}, f32[768,1024]{1,0:T(8,128)}, u32[]{:S(2)}) copy-start(f32[768,1024]{1,0:T(8,128)} %get-tuple-element.3) | copy-start | bytes 9437188
  102.0 2.8 %copy-start.1 = (pred[96,8,4,256]{3,1,2,0:T(8,128)(4,1)S(1)}, pred[96,8,4,256]{3,1,2,0:T(8,128)(4,1)}, u32[]{:S(2)}) copy-start(pred[96,8,4,256]{3,1,2,0:T(8,128)(4,1)} %copy.14) | copy-start | bytes 2359300
  105.8 1.2 copy-start.4
  105.8 1.4 copy-start.6
Sparse Core Ops, SparseCore 0:
  53.3 22.5 all-reduce.5
  80.4 73.5 all-reduce.3
where the time goes:
time: 163 us
  waiting for transfers between devices  83.6 us (51%)
  blocking collectives  21.7 us (13%)
  between operations  14.3 us (9%)
  other arithmetic  14 us (9%)
  starting transfers between devices  10.9 us (7%)
  local copies, waits for them, and re-layouts  10.8 us (7%)
  matrix products  7.4 us (5%)
    psum x1, waiting for transfers between devices, shards(): total3, mass3 = lax.psum((num3, weight3), 'dp')  44.7 us
    psum x1, blocking collectives, shards(): total3, mass3 = lax.psum((num3, weight3), 'dp')  21.7 us
    psum x1, waiting for transfers between devices, shards(): scores = lax.psum(partial_value, 'mp') * scale  19.6 us
    all_to_all x1, waiting for transfers between devices, shards(): lax.all_to_all(sent_rows.reshape(groups, cap, half), 'dp', split_axis=0,...  16.2 us
    all_to_all x1, starting transfers between devices, shards(): lax.all_to_all(sent_labels.reshape(groups, cap), 'dp', split_axis=0, conc...  7.25 us
    all_to_all x1, starting transfers between devices, shards(): lax.all_to_all(sent_rows.reshape(groups, cap, half), 'dp', split_axis=0,...  3.55 us
    scatter x1, local copies, waits for them, and re-layouts, shards(): jnp.zeros((slots, half), jnp.bfloat16).at[target].set(embeddings)  3.33 us
  transfers between devices with their start and end apart: 4, of which 4 were waited for; matrix products, arithmetic and copies ran while one was open for 10% of the time, Pallas kernels for 0%

commit v1 on v0

--- a/solution.py
+++ b/solution.py
@@ -1,6 +1,10 @@
+import functools
+
 import jax
 import jax.numpy as jnp
 from jax import lax
+from jax.experimental import pallas as pl
+from jax.experimental.pallas import tpu as pltpu
 from jax.sharding import PartitionSpec as P
 
 E = 1024
@@ -16,7 +20,7 @@
     return (expd / total).astype(jnp.bfloat16)
 
 
-def shards(embeddings, labels, block_lists, level1, level2, level3):
+def plain_shards(embeddings, labels, block_lists, level1, level2, level3):
     scale = float(E) ** (-0.5)
     groups = lax.axis_size("dp")
     rows, half = embeddings.shape
@@ -73,6 +77,326 @@
     return (new_level1, new_level2, new_level3)
 
 
+MESH = pl.DeviceIdType.MESH
+NT = (((1,), (1,)), ((), ()))
+
+
+def dot_nt(a, b):
+    return lax.dot_general(a, b, NT, preferred_element_type=jnp.float32)
+
+
+def dot_nn(a, b):
+    return jnp.dot(a, b, preferred_element_type=jnp.float32)
+
+
+def partner_order(groups):
+    half = groups // 2
+    order = []
+    for step in range(half):
+        for offset in (half + step, half - step):
+            if 0 < offset < groups and offset not in order:
+                order.append(offset)
+    return [0] + order
+
+
+def step_kernel(
+    groups, cap, emb, lab, lists, l1, l2, l3, o1, o2, o3,
+    sent, sent_lab, got, got_peer, got_lab, l1_peer, l3_peer, half_norm, half_norm3,
+    num, mass, sums, count, listed, n2, n2_peer, part3, w3, got3, got_w3, n3,
+    one_send, one_recv, row_send, row_recv, lab_send, lab_recv, fwd_send, fwd_recv,
+    sum_send, sum_recv, w_send, w_recv, end_send, end_recv,
+):
+    me = lax.axis_index("dp")
+    other = 1 - lax.axis_index("mp")
+    rows = emb.shape[0]
+    k2 = l2.shape[0]
+    k3 = l3.shape[0]
+    k1 = l1.shape[0]
+    seg = k3 // groups
+    scale = float(E) ** (-0.5)
+    order = partner_order(groups)
+
+    def to_owner(offset):
+        return lax.rem(me + offset, groups)
+
+    barrier = pltpu.get_barrier_semaphore()
+    for offset in range(1, groups):
+        pl.semaphore_signal(barrier, inc=1, device_id={"dp": to_owner(offset)}, device_id_type=MESH)
+    pl.semaphore_signal(barrier, inc=1, device_id={"mp": other}, device_id_type=MESH)
+
+    label = lab[...]
+    at = me + lax.broadcasted_iota(jnp.int32, (groups, rows), 0)
+    first = jnp.where(at >= groups, at - groups, at) * k2
+    here = (label >= first) & (label < first + k2)
+    upper = lax.broadcasted_iota(jnp.int32, (rows, rows), 0) <= lax.broadcasted_iota(
+        jnp.int32, (rows, rows), 1
+    )
+    upper = jnp.where(upper, 1.0, 0.0).astype(jnp.bfloat16)
+    cum = dot_nn(jnp.where(here, 1.0, 0.0).astype(jnp.bfloat16), upper).astype(jnp.int32)
+    key = jnp.where(here, cum - 1, -1)
+    local = jnp.where(here, label - first + 1, 0).astype(jnp.float32)
+
+    def peer_copy(src, dst, index):
+        return pltpu.make_async_remote_copy(
+            src_ref=src, dst_ref=dst, send_sem=one_send.at[index], recv_sem=one_recv.at[index],
+            device_id={"mp": other}, device_id_type=MESH,
+        )
+
+    def row_copy(slot, offset):
+        return pltpu.make_async_remote_copy(
+            src_ref=sent.at[slot], dst_ref=got.at[slot],
+            send_sem=row_send.at[slot], recv_sem=row_recv.at[slot],
+            device_id={"dp": to_owner(offset)}, device_id_type=MESH,
+        )
+
+    def lab_copy(slot, offset):
+        return pltpu.make_async_remote_copy(
+            src_ref=sent_lab.at[slot], dst_ref=got_lab.at[slot],
+            send_sem=lab_send.at[slot], recv_sem=lab_recv.at[slot],
+            device_id={"dp": to_owner(offset)}, device_id_type=MESH,
+        )
+
+    def forward(slot):
+        return pltpu.make_async_remote_copy(
+            src_ref=got.at[slot], dst_ref=got_peer.at[slot],
+            send_sem=fwd_send.at[slot], recv_sem=fwd_recv.at[slot],
+            device_id={"mp": other}, device_id_type=MESH,
+        )
+
+    def route(slot):
+        offset = order[slot]
+        spot = lax.broadcasted_iota(jnp.int32, (128, rows), 0) == key[offset : offset + 1]
+        spot = jnp.where(spot, 1.0, 0.0).astype(jnp.bfloat16)
+        names = jnp.broadcast_to(local[offset : offset + 1], (8, rows)).astype(jnp.bfloat16)
+        return dot_nn(spot[:cap], emb[...]).astype(jnp.bfloat16), dot_nt(names, spot)
+
+    for slot in range(1, groups):
+        block, names = route(slot)
+        sent[slot] = block
+        sent_lab[slot] = names
+        if slot == 1:
+            pl.semaphore_wait(barrier, groups)
+        lab_copy(slot, order[slot]).start()
+        row_copy(slot, order[slot]).start()
+    l1_copy = peer_copy(l1, l1_peer, 0)
+    l3_copy = peer_copy(l3, l3_peer, 1)
+    block, names = route(0)
+    got[0] = block
+    got_lab[0] = names
+    forward(0).start()
+    l1_copy.start()
+    l3_copy.start()
+
+    block_of = lax.broadcasted_iota(jnp.int32, (16, k2), 0)
+    hit = lists[0:1] == block_of
+    for entry in range(1, lists.shape[0]):
+        hit = hit | (lists[entry : entry + 1] == block_of)
+    listed[...] = jnp.where(hit, 1.0, 0.0).astype(jnp.bfloat16)
+    num[...] = jnp.zeros_like(num)
+    mass[...] = jnp.zeros_like(mass)
+    sums[...] = jnp.zeros_like(sums)
+    count[...] = jnp.zeros_like(count)
+
+    def own_norms(x):
+        x = x.astype(jnp.float32)
+        return 0.5 * jnp.sum(x * x, axis=1, keepdims=True)
+
+    half_norm[...] = own_norms(l1[...])
+    norms3 = own_norms(l3[...])
+    l1_copy.wait()
+    l3_copy.wait()
+    half_norm[...] += own_norms(l1_peer[...])
+    norms3 = norms3 + own_norms(l3_peer[...])
+    half_norm3[...] = jnp.broadcast_to(norms3, (k3, 128)).T
+
+    def hot(slot):
+        names = got_lab[slot][0:1, :cap].astype(jnp.int32) - 1
+        return lax.broadcasted_iota(jnp.int32, (k2, cap), 0) == names
+
+    def level2_part(slot):
+        member = jnp.where(hot(slot), 1.0, 0.0)
+        sums[...] += dot_nn(member.astype(jnp.bfloat16), got[slot])
+        count[...] += member
+
+    def level1_part(slot):
+        own = got[slot]
+        peer = got_peer[slot]
+        member = jnp.where(hot(slot), 1.0, 0.0).astype(jnp.bfloat16)
+        allowed = dot_nn(listed[...], member)
+        top = jnp.full((1, cap), -1e30, jnp.float32)
+        scores = []
+        masks = []
+        for b in range(BLK_DEV):
+            span = pl.ds(b * BR, BR)
+            score = (dot_nt(l1[span], own) + dot_nt(l1_peer[span], peer) - half_norm[span]) * scale
+            mask = jnp.broadcast_to(allowed[b : b + 1], (BR, cap)) > 0.5
+            top = jnp.maximum(top, jnp.max(jnp.where(mask, score, -1e30), axis=0, keepdims=True))
+            scores.append(score)
+            masks.append(mask)
+        total = jnp.zeros((1, cap), jnp.float32)
+        for b in range(BLK_DEV):
+            scores[b] = jnp.where(masks[b], jnp.exp(scores[b] - top), 0.0)
+            total = total + jnp.sum(scores[b], axis=0, keepdims=True)
+        inverse = 1.0 / jnp.where(total > 0, total, 1.0)
+        for b in range(BLK_DEV):
+            span = pl.ds(b * BR, BR)
+            resp = (scores[b] * inverse).astype(jnp.bfloat16)
+            num[span] += dot_nn(resp, own)
+            mass[span] += resp.astype(jnp.float32)
+
+    level2_part(0)
+
+    def one_slot(slot, carry):
+        lab_copy(slot, 0).wait_recv()
+        row_copy(slot, 0).wait_recv()
+        forward(slot).start()
+        level2_part(slot)
+        forward(slot - 1).wait_recv()
+        level1_part(slot - 1)
+        return carry
+
+    lax.fori_loop(1, groups - 1, one_slot, 0)
+    last = groups - 1
+    lab_copy(last, 0).wait_recv()
+    row_copy(last, 0).wait_recv()
+    forward(last).start()
+    level2_part(last)
+    members = jnp.sum(count[...], axis=1, keepdims=True)
+    new2 = ((sums[...] + l2[...].astype(jnp.float32)) / (members + 1.0)).astype(jnp.bfloat16)
+    n2[...] = new2
+    n2_copy = peer_copy(n2, n2_peer, 2)
+    n2_copy.start()
+    o2[...] = new2
+    forward(last - 1).wait_recv()
+    level1_part(last - 1)
+    n2_copy.wait()
+
+    scores3 = dot_nt(n2[...], l3[...]) + dot_nt(n2_peer[...], l3_peer[...])
+    norm_row = half_norm3[...]
+    scores3 = (scores3 - norm_row[0:1]) * scale
+    top3 = jnp.max(scores3, axis=1, keepdims=True)
+    exp3 = jnp.exp(scores3 - top3)
+    resp3 = exp3 / jnp.sum(exp3, axis=1, keepdims=True)
+    resp3 = resp3.astype(jnp.bfloat16).astype(jnp.float32)
+    part3[...] = dot_nn(resp3.T.astype(jnp.bfloat16), n2[...])
+    w3[...] = jnp.broadcast_to(jnp.sum(resp3, axis=0, keepdims=True), (8, k3))
+
+    def share(owner):
+        return pl.ds(pl.multiple_of(owner * seg, seg), seg)
+
+    def sum_copy(slot, offset):
+        return pltpu.make_async_remote_copy(
+            src_ref=part3.at[share(to_owner(offset))], dst_ref=got3.at[slot],
+            send_sem=sum_send.at[slot], recv_sem=sum_recv.at[slot],
+            device_id={"dp": to_owner(offset)}, device_id_type=MESH,
+        )
+
+    def w_copy(slot, offset):
+        return pltpu.make_async_remote_copy(
+            src_ref=w3, dst_ref=got_w3.at[slot],
+            send_sem=w_send.at[slot], recv_sem=w_recv.at[slot],
+            device_id={"dp": to_owner(offset)}, device_id_type=MESH,
+        )
+
+    def end_copy(slot, offset):
+        return pltpu.make_async_remote_copy(
+            src_ref=n3.at[share(me)], dst_ref=n3.at[share(me)],
+            send_sem=end_send.at[slot], recv_sem=end_recv.at[slot],
+            device_id={"dp": to_owner(offset)}, device_id_type=MESH,
+        )
+
+    for slot in range(1, groups):
+        w_copy(slot, order[slot]).start()
+        sum_copy(slot, order[slot]).start()
+
+    forward(last).wait_recv()
+    level1_part(last)
+    for b in range(BLK_DEV):
+        span = pl.ds(b * BR, BR)
+        weight = jnp.sum(mass[span], axis=1, keepdims=True)
+        o1[span] = ((num[span] + l1[span].astype(jnp.float32)) / (weight + 1.0)).astype(jnp.bfloat16)
+
+    total3 = part3[share(me)]
+    mass3 = w3[...]
+    for slot in range(1, groups):
+        w_copy(slot, order[slot]).wait_recv()
+        sum_copy(slot, order[slot]).wait_recv()
+        total3 = total3 + got3[slot]
+        mass3 = mass3 + got_w3[slot]
+    mine = lax.broadcasted_iota(jnp.int32, (seg, k3), 1) == me * seg + lax.broadcasted_iota(
+        jnp.int32, (seg, k3), 0
+    )
+    mass_own = jnp.sum(jnp.where(mine, mass3[0:1], 0.0), axis=1, keepdims=True)
+    new3 = (total3 + l3[share(me)].astype(jnp.float32)) / (mass_own + 1.0)
+    n3[share(me)] = new3.astype(jnp.bfloat16)
+    for slot in range(1, groups):
+        end_copy(slot, order[slot]).start()
+    for slot in range(1, groups):
+        lab_copy(slot, order[slot]).wait_send()
+        row_copy(slot, order[slot]).wait_send()
+        w_copy(slot, order[slot]).wait_send()
+        sum_copy(slot, order[slot]).wait_send()
+    for slot in range(groups):
+        forward(slot).wait_send()
+    for slot in range(1, groups):
+        end_copy(slot, order[slot]).wait_recv()
+    o3[...] = n3[...]
+    for slot in range(1, groups):
+        end_copy(slot, order[slot]).wait_send()
+
+
+def shards(embeddings, labels, block_lists, level1, level2, level3):
+    groups = lax.axis_size("dp")
+    rows, half = embeddings.shape
+    k1, k2, k3 = level1.shape[0], level2.shape[0], level3.shape[0]
+    cap = max(2, 2 * rows // groups)
+    if cap % 16 or cap > 128 or groups % 8 or k3 % (16 * groups):
+        return plain_shards(embeddings, labels, block_lists, level1, level2, level3)
+    vmem = pl.BlockSpec(memory_space=pltpu.VMEM)
+    bf16, f32 = jnp.bfloat16, jnp.float32
+    dma = pltpu.SemaphoreType.DMA
+    seg = k3 // groups
+    return pl.pallas_call(
+        functools.partial(step_kernel, groups, cap),
+        out_shape=(
+            jax.ShapeDtypeStruct((k1, half), bf16),
+            jax.ShapeDtypeStruct((k2, half), bf16),
+            jax.ShapeDtypeStruct((k3, half), bf16),
+        ),
+        in_specs=[vmem] * 6,
+        out_specs=(vmem,) * 3,
+        scratch_shapes=[
+            pltpu.VMEM((groups, cap, half), bf16),
+            pltpu.VMEM((groups, 8, 128), f32),
+            pltpu.VMEM((groups, cap, half), bf16),
+            pltpu.VMEM((groups, cap, half), bf16),
+            pltpu.VMEM((groups, 8, 128), f32),
+            pltpu.VMEM((k1, half), bf16),
+            pltpu.VMEM((k3, half), bf16),
+            pltpu.VMEM((k1, 1), f32),
+            pltpu.VMEM((128, k3), f32),
+            pltpu.VMEM((k1, half), f32),
+            pltpu.VMEM((k1, cap), f32),
+            pltpu.VMEM((k2, half), f32),
+            pltpu.VMEM((k2, cap), f32),
+            pltpu.VMEM((16, k2), bf16),
+            pltpu.VMEM((k2, half), bf16),
+            pltpu.VMEM((k2, half), bf16),
+            pltpu.VMEM((k3, half), f32),
+            pltpu.VMEM((8, k3), f32),
+            pltpu.VMEM((groups, seg, half), f32),
+            pltpu.VMEM((groups, 8, k3), f32),
+            pltpu.VMEM((k3, half), bf16),
+            dma((3,)),
+            dma((3,)),
+        ]
+        + [dma((groups,))] * 12,
+        compiler_params=pltpu.CompilerParams(
+            collective_id=0, has_side_effects=True, vmem_limit_bytes=40 * 1024 * 1024
+        ),
+    )(embeddings, labels.reshape(1, rows), block_lists.T, level1, level2, level3)
+
+
 def solution(mesh):
     return jax.shard_map(
         shards,

time: 163 us -> 61.8 us (0.38)
  waiting for transfers between devices: 83.6 us -> 0 us
  Pallas kernels: 0 us -> 53.8 us
  blocking collectives: 21.7 us -> 0 us
  other arithmetic: 14 us -> 0 us
  between operations: 14.3 us -> 0.65 us
  starting transfers between devices: 10.9 us -> 0 us
  matrix products: 7.4 us -> 0 us
  local copies, waits for them, and re-layouts: 10.8 us -> 7.1 us
    psum x2 -> x0, waiting for transfers between devices: 64.4 us -> none  [the longest x1 44.7 us: shards(): total3, mass3 = lax.psum((num3, weight3), 'dp')]
    pallas_call x0 -> x1, Pallas kernels: none -> 53.8 us  [shards(): pl.pallas_call(functools.partial(step_kernel, groups, cap), out_shape=(ja...]
    psum x1 -> x0, blocking collectives: 21.7 us -> none  [shards(): total3, mass3 = lax.psum((num3, weight3), 'dp')]
    all_to_all x2 -> x0, waiting for transfers between devices: 19.2 us -> none  [the longest x1 16.2 us: shards(): lax.all_to_all(sent_rows.reshape(groups, cap, half), 'dp', split_axis=0,...]
    all_to_all x2 -> x0, starting transfers between devices: 10.8 us -> none  [the longest x1 7.25 us: shards(): lax.all_to_all(sent_labels.reshape(groups, cap), 'dp', split_axis=0, conc...]
    dot_general x6 -> x0, matrix products: 7.4 us -> none  [the longest x1 2.71 us: shards(): jnp.dot(got_rows, level1.T, preferred_element_type=jnp.float32)]
    scatter x2 -> x0, local copies, waits for them, and re-layouts: 6.26 us -> none  [the longest x1 3.33 us: shards(): jnp.zeros((slots, half), jnp.bfloat16).at[target].set(embeddings)]
    reduce_sum x8 -> x0, other arithmetic: 5.81 us -> none  [the longest x1 1.09 us: shards(): resp3 = jax.nn.softmax(scores3, axis=1).astype(jnp.bfloat16)]
  transfers between devices with their start and end apart: 4 -> 0, of which waited for: 4 -> 0; matrix products, arithmetic and copies ran while one was open for 10% -> 0% of each run, Pallas kernels for 0% -> 0%
where the time goes in v1:
time: 61.8 us; the launch traced here: 61.5 us
  Pallas kernels  53.8 us (87%)
  local copies, waits for them, and re-layouts  7.1 us (11%)
  between operations  0.65 us (1%)
    pallas_call x1, Pallas kernels, shards(): pl.pallas_call(functools.partial(step_kernel, groups, cap), out_shape=(ja...  53.8 us
    unnamed x13, local copies, waits for them, and re-layouts  6.41 us

profile of v1, /device:TPU:0, one launch (start us, length us, event | category | flops | bytes accessed | tf_op | source)
XLA Modules:
  0.0 61.5 jit_solution(3127324756103736481)
XLA Ops:
  0.6 0.0 copy-start.4
  0.6 0.7 %reshape.9.lab = s32[1,384]{1,0:T(1,128)S(1)} reshape(s32[384]{0:T(512)} %param.7) | data formatting | bytes 3072 | tf_op jit(solution)/shard_map/reshape | solution.py:397
  1.3 0.0 copy-done.4
  1.3 0.0 copy-start
  1.3 1.2 %copy-done = bf16[1024,512]{1,0:T(8,128)(2,1)S(1)} copy-done((bf16[1024,512]{1,0:T(8,128)(2,1)S(1)}, bf16[1024,512]{1,0:T(8,128)(2,1)}, u32[]{:S(2)}) %copy-start) | copy-done | bytes 1048600
  2.6 0.0 copy-start.1
  2.6 1.0 %copy-done.1 = bf16[384,512]{1,0:T(8,128)(2,1)S(1)} copy-done((bf16[384,512]{1,0:T(8,128)(2,1)S(1)}, bf16[384,512]{1,0:T(8,128)(2,1)}, u32[]{:S(2)}) %copy-start.1) | copy-done | bytes 393240
  3.6 0.0 copy-start.2
  3.6 0.9 %copy-done.2 = bf16[256,512]{1,0:T(8,128)(2,1)S(1)} copy-done((bf16[256,512]{1,0:T(8,128)(2,1)S(1)}, bf16[256,512]{1,0:T(8,128)(2,1)}, u32[]{:S(2)}) %copy-start.2) | copy-done | bytes 262168
  4.5 0.0 copy-start.3
  4.5 0.9 %copy-done.3 = bf16[128,512]{1,0:T(8,128)(2,1)S(1)} copy-done((bf16[128,512]{1,0:T(8,128)(2,1)S(1)}, bf16[128,512]{1,0:T(8,128)(2,1)}, u32[]{:S(2)}) %copy-start.3) | copy-done | bytes 131096
  5.4 53.8 %shard_map.85 = (bf16[1024,512]{1,0:T(8,128)(2,1)S(1)}, bf16[128,512]{1,0:T(8,128)(2,1)S(1)}, bf16[256,512]{1,0:T(8,128)(2,1)S(1)}) custom-call(bf16[384,512]{1,0:T(8,128)(2,1)S(1)} %copy-done.1, s32[1,384]{1,0:T(1,128)S(1)} %reshape.9.lab, s32[2,128]{1,0:T(2,128)S(1)} %bitcast.1, bf16[1024,512]{1,0:T(8,128)(2,1)S(1)} %copy-done, ...), custom_call_target="tpu_custom_call" | custom-call | tf_op jit(solution)/shard_map/pallas_call | solution.py:359
  59.2 1.0 %copy.12 = bf16[1024,512]{1,0:T(8,128)(2,1)} copy(bf16[1024,512]{1,0:T(8,128)(2,1)S(1)} %get-tuple-element.6) | data formatting | bytes 2097152
  60.2 0.7 %copy.13 = bf16[128,512]{1,0:T(8,128)(2,1)} copy(bf16[128,512]{1,0:T(8,128)(2,1)S(1)} %get-tuple-element.7) | data formatting | bytes 262144
  60.8 0.7 %copy.14 = bf16[256,512]{1,0:T(8,128)(2,1)} copy(bf16[256,512]{1,0:T(8,128)(2,1)S(1)} %get-tuple-element.8) | data formatting | bytes 524288
Async XLA Ops:
  0.6 0.7 %copy-start.4 = (s32[128,2]{0,1:T(2,128)S(1)}, s32[128,2]{0,1:T(2,128)}, u32[]{:S(2)}) copy-start(s32[128,2]{0,1:T(2,128)} %param.8) | copy-start | bytes 3076
  1.3 1.2 %copy-start = (bf16[1024,512]{1,0:T(8,128)(2,1)S(1)}, bf16[1024,512]{1,0:T(8,128)(2,1)}, u32[]{:S(2)}) copy-start(bf16[1024,512]{1,0:T(8,128)(2,1)} %l1.1) | copy-start | bytes 3145732
  2.6 1.0 %copy-start.1 = (bf16[384,512]{1,0:T(8,128)(2,1)S(1)}, bf16[384,512]{1,0:T(8,128)(2,1)}, u32[]{:S(2)}) copy-start(bf16[384,512]{1,0:T(8,128)(2,1)} %emb.1) | copy-start | bytes 1179652
  3.6 0.9 %copy-start.2 = (bf16[256,512]{1,0:T(8,128)(2,1)S(1)}, bf16[256,512]{1,0:T(8,128)(2,1)}, u32[]{:S(2)}) copy-start(bf16[256,512]{1,0:T(8,128)(2,1)} %l3.1) | copy-start | bytes 786436
  4.5 0.9 %copy-start.3 = (bf16[128,512]{1,0:T(8,128)(2,1)S(1)}, bf16[128,512]{1,0:T(8,128)(2,1)}, u32[]{:S(2)}) copy-start(bf16[128,512]{1,0:T(8,128)(2,1)} %l2.1) | copy-start | bytes 393220

commit v2 on v1

--- a/solution.py
+++ b/solution.py
@@ -96,11 +96,12 @@
         for offset in (half + step, half - step):
             if 0 < offset < groups and offset not in order:
                 order.append(offset)
-    return [0] + order
+    return [0] + order[::-1]
 
 
 def step_kernel(
-    groups, cap, emb, lab, lists, l1, l2, l3, o1, o2, o3,
+    groups, cap, emb_hbm, lab_ref, lists, l1_hbm, l2_hbm, l3_hbm, o1_hbm, o2_hbm, o3_hbm,
+    emb, l1, l2, l3, part3_own, o1, in_sem, out_sem,
     sent, sent_lab, got, got_peer, got_lab, l1_peer, l3_peer, half_norm, half_norm3,
     num, mass, sums, count, listed, n2, n2_peer, part3, w3, got3, got_w3, n3,
     one_send, one_recv, row_send, row_recv, lab_send, lab_recv, fwd_send, fwd_recv,
@@ -119,12 +120,24 @@
     def to_owner(offset):
         return lax.rem(me + offset, groups)
 
+    def load(src, dst, index):
+        return pltpu.make_async_copy(src, dst, in_sem.at[index])
+
+    emb_load = load(emb_hbm, emb, 0)
+    l1_load = load(l1_hbm, l1, 1)
+    l2_load = load(l2_hbm, l2, 2)
+    l3_load = load(l3_hbm, l3, 3)
+    emb_load.start()
     barrier = pltpu.get_barrier_semaphore()
     for offset in range(1, groups):
         pl.semaphore_signal(barrier, inc=1, device_id={"dp": to_owner(offset)}, device_id_type=MESH)
     pl.semaphore_signal(barrier, inc=1, device_id={"mp": other}, device_id_type=MESH)
 
-    label = lab[...]
+    l1_load.start()
+    l3_load.start()
+    l2_load.start()
+
+    label = lab_ref[...].reshape(1, rows)
     at = me + lax.broadcasted_iota(jnp.int32, (groups, rows), 0)
     first = jnp.where(at >= groups, at - groups, at) * k2
     here = (label >= first) & (label < first + k2)
@@ -168,8 +181,9 @@
         spot = lax.broadcasted_iota(jnp.int32, (128, rows), 0) == key[offset : offset + 1]
         spot = jnp.where(spot, 1.0, 0.0).astype(jnp.bfloat16)
         names = jnp.broadcast_to(local[offset : offset + 1], (8, rows)).astype(jnp.bfloat16)
-        return dot_nn(spot[:cap], emb[...]).astype(jnp.bfloat16), dot_nt(names, spot)
-
+        return dot_nn(spot[:cap], emb[...]).astype(jnp.bfloat16), dot_nt(names, spot)[0:1]
+
+    emb_load.wait()
     for slot in range(1, groups):
         block, names = route(slot)
         sent[slot] = block
@@ -178,8 +192,8 @@
             pl.semaphore_wait(barrier, groups)
         lab_copy(slot, order[slot]).start()
         row_copy(slot, order[slot]).start()
-    l1_copy = peer_copy(l1, l1_peer, 0)
-    l3_copy = peer_copy(l3, l3_peer, 1)
+    l1_copy = peer_copy(l1_hbm, l1_peer, 0)
+    l3_copy = peer_copy(l3_hbm, l3_peer, 1)
     block, names = route(0)
     got[0] = block
     got_lab[0] = names
@@ -201,6 +215,9 @@
         x = x.astype(jnp.float32)
         return 0.5 * jnp.sum(x * x, axis=1, keepdims=True)
 
+    l1_load.wait()
+    l3_load.wait()
+    l2_load.wait()
     half_norm[...] = own_norms(l1[...])
     norms3 = own_norms(l3[...])
     l1_copy.wait()
@@ -266,7 +283,8 @@
     n2[...] = new2
     n2_copy = peer_copy(n2, n2_peer, 2)
     n2_copy.start()
-    o2[...] = new2
+    o2_copy = pltpu.make_async_copy(n2, o2_hbm, out_sem.at[BLK_DEV])
+    o2_copy.start()
     forward(last - 1).wait_recv()
     level1_part(last - 1)
     n2_copy.wait()
@@ -278,8 +296,10 @@
     exp3 = jnp.exp(scores3 - top3)
     resp3 = exp3 / jnp.sum(exp3, axis=1, keepdims=True)
     resp3 = resp3.astype(jnp.bfloat16).astype(jnp.float32)
-    part3[...] = dot_nn(resp3.T.astype(jnp.bfloat16), n2[...])
-    w3[...] = jnp.broadcast_to(jnp.sum(resp3, axis=0, keepdims=True), (8, k3))
+    sum3 = dot_nn(resp3.T.astype(jnp.bfloat16), n2[...])
+    part3[...] = sum3.astype(jnp.bfloat16)
+    part3_own[...] = sum3
+    w3[...] = jnp.sum(resp3, axis=0, keepdims=True)
 
     def share(owner):
         return pl.ds(pl.multiple_of(owner * seg, seg), seg)
@@ -311,22 +331,26 @@
 
     forward(last).wait_recv()
     level1_part(last)
+    o1_copies = []
     for b in range(BLK_DEV):
         span = pl.ds(b * BR, BR)
         weight = jnp.sum(mass[span], axis=1, keepdims=True)
         o1[span] = ((num[span] + l1[span].astype(jnp.float32)) / (weight + 1.0)).astype(jnp.bfloat16)
-
-    total3 = part3[share(me)]
+        copy = pltpu.make_async_copy(o1.at[span], o1_hbm.at[span], out_sem.at[b])
+        copy.start()
+        o1_copies.append(copy)
+
+    total3 = part3_own[share(me)]
     mass3 = w3[...]
     for slot in range(1, groups):
         w_copy(slot, order[slot]).wait_recv()
         sum_copy(slot, order[slot]).wait_recv()
-        total3 = total3 + got3[slot]
+        total3 = total3 + got3[slot].astype(jnp.float32)
         mass3 = mass3 + got_w3[slot]
     mine = lax.broadcasted_iota(jnp.int32, (seg, k3), 1) == me * seg + lax.broadcasted_iota(
         jnp.int32, (seg, k3), 0
     )
-    mass_own = jnp.sum(jnp.where(mine, mass3[0:1], 0.0), axis=1, keepdims=True)
+    mass_own = jnp.sum(jnp.where(mine, mass3, 0.0), axis=1, keepdims=True)
     new3 = (total3 + l3[share(me)].astype(jnp.float32)) / (mass_own + 1.0)
     n3[share(me)] = new3.astype(jnp.bfloat16)
     for slot in range(1, groups):
@@ -340,9 +364,33 @@
         forward(slot).wait_send()
     for slot in range(1, groups):
         end_copy(slot, order[slot]).wait_recv()
-    o3[...] = n3[...]
+    o3_copy = pltpu.make_async_copy(n3, o3_hbm, out_sem.at[BLK_DEV + 1])
+    o3_copy.start()
+    for copy in o1_copies:
+        copy.wait()
+    o2_copy.wait()
     for slot in range(1, groups):
         end_copy(slot, order[slot]).wait_send()
+    o3_copy.wait()
+
+
+def write_kernel(a, b, c, a_out, b_out, c_out, a_mid, b_mid, c_mid, in_sem, out_sem):
+    pieces = []
+    for index in range(BLK_DEV):
+        span = pl.ds(index * BR, BR)
+        pieces.append((a.at[span], a_mid.at[span], a_out.at[span]))
+    pieces += [(b, b_mid, b_out), (c, c_mid, c_out)]
+    reads, writes = [], []
+    for index, (src, mid, dst) in enumerate(pieces):
+        reads.append(pltpu.make_async_copy(src, mid, in_sem.at[index]))
+        writes.append(pltpu.make_async_copy(mid, dst, out_sem.at[index]))
+    for read in reads:
+        read.start()
+    for read, write in zip(reads, writes):
+        read.wait()
+        write.start()
+    for write in writes:
+        write.wait()
 
 
 def shards(embeddings, labels, block_lists, level1, level2, level3):
@@ -353,24 +401,33 @@
     if cap % 16 or cap > 128 or groups % 8 or k3 % (16 * groups):
         return plain_shards(embeddings, labels, block_lists, level1, level2, level3)
     vmem = pl.BlockSpec(memory_space=pltpu.VMEM)
+    hbm = pl.BlockSpec(memory_space=pltpu.HBM)
     bf16, f32 = jnp.bfloat16, jnp.float32
     dma = pltpu.SemaphoreType.DMA
     seg = k3 // groups
-    return pl.pallas_call(
+    outs = pl.pallas_call(
         functools.partial(step_kernel, groups, cap),
         out_shape=(
             jax.ShapeDtypeStruct((k1, half), bf16),
             jax.ShapeDtypeStruct((k2, half), bf16),
             jax.ShapeDtypeStruct((k3, half), bf16),
         ),
-        in_specs=[vmem] * 6,
-        out_specs=(vmem,) * 3,
+        in_specs=[hbm, vmem, vmem, hbm, hbm, hbm],
+        out_specs=(hbm,) * 3,
         scratch_shapes=[
+            pltpu.VMEM((rows, half), bf16),
+            pltpu.VMEM((k1, half), bf16),
+            pltpu.VMEM((k2, half), bf16),
+            pltpu.VMEM((k3, half), bf16),
+            pltpu.VMEM((k3, half), f32),
+            pltpu.VMEM((k1, half), bf16),
+            dma((4,)),
+            dma((BLK_DEV + 2,)),
             pltpu.VMEM((groups, cap, half), bf16),
-            pltpu.VMEM((groups, 8, 128), f32),
+            pltpu.VMEM((groups, 1, 128), f32),
             pltpu.VMEM((groups, cap, half), bf16),
             pltpu.VMEM((groups, cap, half), bf16),
-            pltpu.VMEM((groups, 8, 128), f32),
+            pltpu.VMEM((groups, 1, 128), f32),
             pltpu.VMEM((k1, half), bf16),
             pltpu.VMEM((k3, half), bf16),
             pltpu.VMEM((k1, 1), f32),
@@ -382,19 +439,28 @@
             pltpu.VMEM((16, k2), bf16),
             pltpu.VMEM((k2, half), bf16),
             pltpu.VMEM((k2, half), bf16),
-            pltpu.VMEM((k3, half), f32),
-            pltpu.VMEM((8, k3), f32),
-            pltpu.VMEM((groups, seg, half), f32),
-            pltpu.VMEM((groups, 8, k3), f32),
+            pltpu.VMEM((k3, half), bf16),
+            pltpu.VMEM((1, k3), f32),
+            pltpu.VMEM((groups, seg, half), bf16),
+            pltpu.VMEM((groups, 1, k3), f32),
             pltpu.VMEM((k3, half), bf16),
             dma((3,)),
             dma((3,)),
         ]
         + [dma((groups,))] * 12,
         compiler_params=pltpu.CompilerParams(
-            collective_id=0, has_side_effects=True, vmem_limit_bytes=40 * 1024 * 1024
+            collective_id=0, has_side_effects=True, vmem_limit_bytes=60 * 1024 * 1024
         ),
-    )(embeddings, labels.reshape(1, rows), block_lists.T, level1, level2, level3)
+    )(embeddings, labels, block_lists.T, level1, level2, level3)
+    return pl.pallas_call(
+        write_kernel,
+        out_shape=tuple(jax.ShapeDtypeStruct(out.shape, out.dtype) for out in outs),
+        in_specs=[hbm] * 3,
+        out_specs=(hbm,) * 3,
+        scratch_shapes=[pltpu.VMEM(out.shape, out.dtype) for out in outs]
+        + [dma((BLK_DEV + 2,))] * 2,
+        compiler_params=pltpu.CompilerParams(vmem_limit_bytes=60 * 1024 * 1024),
+    )(*outs)
 
 
 def solution(mesh):

time: 61.8 us -> 46.4 us (0.75)
  Pallas kernels: 53.8 us -> 45.5 us
  local copies, waits for them, and re-layouts: 7.1 us -> 0 us
    pallas_call x1, Pallas kernels: 53.8 us -> 43.4 us  [shards(): pl.pallas_call(functools.partial(step_kernel, groups, cap), out_shape=(ja...]
    unnamed x13 -> x0, local copies, waits for them, and re-layouts: 6.41 us -> none
    pallas_call x0 -> x1, Pallas kernels: none -> 2.15 us  [shards(): pl.pallas_call(write_kernel, out_shape=tuple((jax.ShapeDtypeStruct(out.sh...]
    reshape x1 -> x0, local copies, waits for them, and re-layouts: 0.69 us -> none  [shards(): labels.reshape(1, rows)]
where the time goes in v2:
time: 46.4 us; the launch traced here: 46.2 us
  Pallas kernels  45.5 us (98%)
  between operations  0.64 us (1%)
    pallas_call x1, Pallas kernels, shards(): pl.pallas_call(functools.partial(step_kernel, groups, cap), out_shape=(ja...  43.4 us
    pallas_call x1, Pallas kernels, shards(): pl.pallas_call(write_kernel, out_shape=tuple((jax.ShapeDtypeStruct(out.sh...  2.15 us

profile of v2, /device:TPU:0, one launch (start us, length us, event | category | flops | bytes accessed | tf_op | source)
XLA Modules:
  0.0 46.2 jit_solution(739222871246678804)
XLA Ops:
  0.6 43.4 %shard_map.85 = (bf16[1024,512]{1,0:T(8,128)(2,1)}, bf16[128,512]{1,0:T(8,128)(2,1)}, bf16[256,512]{1,0:T(8,128)(2,1)}) custom-call(bf16[384,512]{1,0:T(8,128)(2,1)} %emb_hbm.1, s32[384]{0:T(512)} %lab_ref.1, s32[2,128]{1,0:T(2,128)} %bitcast.1, bf16[1024,512]{1,0:T(8,128)(2,1)} %l1_hbm.1, bf16[128,512]{1,0:T(8,128)(2,1)} %l2_hbm.1, bf16[256,512]{1,0:T(8,128)(2,1)} %l3_hbm.1), custom_call_target="tpu_custom_call" | custom-call | tf_op jit(solution)/shard_map/pallas_call | solution.py:408
  44.0 2.1 %shard_map.86 = (bf16[1024,512]{1,0:T(8,128)(2,1)}, bf16[128,512]{1,0:T(8,128)(2,1)}, bf16[256,512]{1,0:T(8,128)(2,1)}) custom-call(bf16[1024,512]{1,0:T(8,128)(2,1)} %get-tuple-element.6.a, bf16[128,512]{1,0:T(8,128)(2,1)} %get-tuple-element.7.b, bf16[256,512]{1,0:T(8,128)(2,1)} %get-tuple-element.8.c), custom_call_target="tpu_custom_call" | custom-call | tf_op jit(solution)/shard_map/pallas_call | solution.py:455

commit v3 on v2

--- a/solution.py
+++ b/solution.py
@@ -187,11 +187,11 @@
     for slot in range(1, groups):
         block, names = route(slot)
         sent[slot] = block
-        sent_lab[slot] = names
         if slot == 1:
             pl.semaphore_wait(barrier, groups)
+        row_copy(slot, order[slot]).start()
+        sent_lab[slot] = names
         lab_copy(slot, order[slot]).start()
-        row_copy(slot, order[slot]).start()
     l1_copy = peer_copy(l1_hbm, l1_peer, 0)
     l3_copy = peer_copy(l3_hbm, l3_peer, 1)
     block, names = route(0)

time: 46.4 us -> 46.4 us (level)
  no operation moved by 1% of the time
where the time goes in v3:
time: 46.4 us; the launch traced here: 46.2 us
  Pallas kernels  45.6 us (98%)
  between operations  0.64 us (1%)
    pallas_call x1, Pallas kernels, shards(): pl.pallas_call(functools.partial(step_kernel, groups, cap), out_shape=(ja...  43.5 us
    pallas_call x1, Pallas kernels, shards(): pl.pallas_call(write_kernel, out_shape=tuple((jax.ShapeDtypeStruct(out.sh...  2.15 us

profile of v3, /device:TPU:0, one launch (start us, length us, event | category | flops | bytes accessed | tf_op | source)
XLA Modules:
  0.0 46.2 jit_solution(1297556975960620600)
XLA Ops:
  0.6 43.5 %shard_map.85 = (bf16[1024,512]{1,0:T(8,128)(2,1)}, bf16[128,512]{1,0:T(8,128)(2,1)}, bf16[256,512]{1,0:T(8,128)(2,1)}) custom-call(bf16[384,512]{1,0:T(8,128)(2,1)} %emb_hbm.1, s32[384]{0:T(512)} %lab_ref.1, s32[2,128]{1,0:T(2,128)} %bitcast.1, bf16[1024,512]{1,0:T(8,128)(2,1)} %l1_hbm.1, bf16[128,512]{1,0:T(8,128)(2,1)} %l2_hbm.1, bf16[256,512]{1,0:T(8,128)(2,1)} %l3_hbm.1), custom_call_target="tpu_custom_call" | custom-call | tf_op jit(solution)/shard_map/pallas_call | solution.py:408
  44.1 2.1 %shard_map.86 = (bf16[1024,512]{1,0:T(8,128)(2,1)}, bf16[128,512]{1,0:T(8,128)(2,1)}, bf16[256,512]{1,0:T(8,128)(2,1)}) custom-call(bf16[1024,512]{1,0:T(8,128)(2,1)} %get-tuple-element.6.a, bf16[128,512]{1,0:T(8,128)(2,1)} %get-tuple-element.7.b, bf16[256,512]{1,0:T(8,128)(2,1)} %get-tuple-element.8.c), custom_call_target="tpu_custom_call" | custom-call | tf_op jit(solution)/shard_map/pallas_call | solution.py:455
